TPU v7x, 32 devices: a whole 2x2x4 slice. The times are simulated.
32 devices in a mesh: wide: 8 (over z, x), narrow: 4 (over y, core).
Axes of the slice: x: 2, y: 2, z: 4, core: 2. Of those that a mesh axis runs over, the one named last changes fastest.
Arguments:
- object_field: float32 [2, 2048, 2048], P(None, 'narrow', 'wide'), may hold values from -6 to 6
- probe: float32 [4, 2, 256, 256], replicated, may hold values from -3 to 3
- amplitudes: float32 [256, 256, 256], P(('wide', 'narrow')), may hold values from 0.5 to 4
- offsets: int32 [256, 2], P(('wide', 'narrow')), may hold values from 0 to 1792, as said below
- live: int32 [32], P(('wide', 'narrow')), may hold values from 1 to 8, as said below
Outputs:
- object_grad: float32 [2, 2048, 2048], P(None, 'narrow', 'wide')
- probe_grad: float32 [4, 2, 256, 256], replicated
Inputs may be any that keep to these rules, and one draw needn't show every extreme that they name: `offsets`: the patch of every slot (used or not) lies wholly inside the object, and starts inside the object tile of 512 rows and 256 columns that holds the same mesh place as the slot: slot p with b = p // 8, row tile b % (2048 / 512) and column tile b // (2048 / 512). Block b of 8 slots uses its first live[b] slots; in every draw some block uses all 8.
All inputs are finite; a program needn't handle non-finite values.
Results may differ from a plain program's by a relative error of at most 0.005.
Values sent between devices are 32-bit elements; how exact they have to be, the bound alone decides.
No kernel may reach another device: no remote copies, remote signals or barrier semaphores. Data moves between devices by JAX's collectives and lax.ppermute only.
A program may use at most 128 MiB of HBM per device.

v0:
```python
import functools
import math

import jax
import jax.numpy as jnp
import ml_dtypes
import numpy as np
from jax import lax
from jax.experimental import pallas as pl
from jax.experimental.pallas import tpu as pltpu
from jax.sharding import PartitionSpec as P

F32 = jnp.float32
BF16 = jnp.bfloat16
LANES = 128
PAIR = 2


def half_dft(extent):
    half = extent // 2
    blocks = []
    for parity in range(2):
        freq = 2 * np.arange(half)[:, None] + parity
        angles = (freq * np.arange(half)[None, :] % extent) * (2.0 * math.pi / extent)
        cosine = np.cos(angles) / math.sqrt(extent)
        sine = np.sin(angles) / math.sqrt(extent)
        blocks.append(np.block([[cosine, sine], [-sine, cosine]]))
    both = np.stack(blocks)
    return np.stack([both, np.swapaxes(both, 1, 2)]).astype(ml_dtypes.bfloat16)


def parity_order(extent):
    order = np.concatenate([np.arange(0, extent, 2), np.arange(1, extent, 2)])
    matrix = np.zeros((extent, extent), np.float32)
    matrix[order, np.arange(extent)] = 1.0
    return matrix


def dot(a, b):
    return jnp.dot(a, b, preferred_element_type=F32)


def slots_kernel(
    tile_rows, tile_cols, offsets, live, own, below, right, right_low, corner, probe_in, amps, mats, order,
    grad_own, grad_below, grad_right, grad_right_low, grad_corner, probe_keep, probe_send,
    ext, grad, probe, probe_sum, window, part, amp, sorted_amp, waves, inner, far, power, across,
    in_sems, amp_sems, out_sems,
):
    modes = probe.shape[0]
    extent = probe.shape[2]
    half = extent // 2
    rows_step = 32
    wide_cols = extent // LANES + 1
    count = live[0]

    low_rows = slice(tile_rows, tile_rows + extent)
    whole = slice(0, tile_cols)
    rim = slice(tile_cols, tile_cols + extent)
    places = [
        (own, slice(0, tile_rows), whole),
        (below, low_rows, whole),
        (right, slice(0, extent), rim),
        (right_low, slice(extent, tile_rows), rim),
        (corner, low_rows, rim),
    ]

    def strips(array, rows, cols):
        for start in range(0, cols.stop - cols.start, LANES):
            yield array.at[:, :, start : start + LANES], ((slice(None), (cols.start + start) // LANES, rows, slice(None)))

    strip_loads = [(src, at) for array, rows, cols in places for src, at in strips(array, rows, cols)]
    loads = [pltpu.make_async_copy(src, ext.at[at], in_sems.at[n]) for n, (src, at) in enumerate(strip_loads)]
    loads.append(pltpu.make_async_copy(probe_in, probe, in_sems.at[len(loads)]))
    for load in loads:
        load.start()
    grad[...] = jnp.zeros_like(grad)
    probe_sum[...] = jnp.zeros_like(probe_sum)
    for load in loads:
        load.wait()
    lane = lax.broadcasted_iota(jnp.int32, (rows_step, LANES), 1)

    def rows_of(k, c, rows):
        start = (k * 2 + c) * extent
        return slice(start + rows.start, start + rows.stop)

    def take(q, row_at, first_tile, shift):
        back = lax.rem(LANES - shift, LANES)
        for plane in range(2):
            for row in range(0, extent, rows_step):
                rows = pl.ds(row_at + row, rows_step)
                turned = [pltpu.roll(ext[plane, first_tile + c, rows, :], back, 1) for c in range(wide_cols)]
                for c in range(wide_cols - 1):
                    window[q, plane, row : row + rows_step, c * LANES : (c + 1) * LANES] = jnp.where(
                        lane < LANES - shift, turned[c], turned[c + 1]
                    )

    def give(q, row_at, first_tile, shift):
        zero = jnp.zeros((rows_step, LANES), F32)
        for plane in range(2):
            for row in range(0, extent, rows_step):
                rows = pl.ds(row_at + row, rows_step)
                turned = [zero]
                for c in range(wide_cols - 1):
                    turned.append(pltpu.roll(part[q, plane, row : row + rows_step, c * LANES : (c + 1) * LANES], shift, 1))
                turned.append(zero)
                for c in range(wide_cols):
                    grad[plane, first_tile + c, rows, :] += jnp.where(lane >= shift, turned[c + 1], turned[c])

    def psi(k):
        for row in range(0, half, rows_step):
            spans = [slice(base, base + rows_step) for base in (row, half + row)]
            probes = [(probe[k, 0, rows, :], probe[k, 1, rows, :]) for rows in spans]
            for q in range(PAIR):
                waves_at = []
                for rows, (pr, pi) in zip(spans, probes):
                    o_re, o_im = window[q, 0, rows, :], window[q, 1, rows, :]
                    waves_at.append((pr * o_re - pi * o_im, pr * o_im + pi * o_re))
                for c in range(2):
                    rows = slice(c * half + row, c * half + row + rows_step)
                    waves[q, k, 0, rows, :] = (waves_at[0][c] + waves_at[1][c]).astype(BF16)
                    waves[q, k, 1, rows, :] = (waves_at[0][c] - waves_at[1][c]).astype(BF16)

    def left(q, k):
        for a in range(2):
            z = dot(mats[0, a], waves[q, k, a])
            left, right_half = z[:, :half], z[:, half:]
            for b, value in enumerate((left + right_half, left - right_half)):
                value = value.astype(BF16)
                inner[q, k, b, a * half : (a + 1) * half, :half] = value[:half]
                inner[q, k, b, a * half : (a + 1) * half, half:] = value[half:]

    def right(q, k):
        for b in range(2):
            f = dot(inner[q, k, b], mats[1, b])
            far[q, k, b] = f
            own_power = f[:, :half] * f[:, :half] + f[:, half:] * f[:, half:]
            power[q, b] = own_power if k == 0 else power[q, b] + own_power

    def factors(q, used):
        high = amp[q].astype(BF16)
        low = (amp[q] - high.astype(F32)).astype(BF16)
        turned = dot(high, order[...]) + dot(low, order[...])
        for b in range(2):
            sorted_amp[q, b] = turned[:, b * half : (b + 1) * half]
        for b in range(2):
            for a in range(2):
                rows = slice(a * half, (a + 1) * half)
                for_rows = sorted_amp[q, b, pl.ds(a, half, 2), :]
                factor = 2.0 - 2.0 * for_rows * lax.rsqrt(power[q, b, rows] + 0.5)
                power[q, b, rows] = factor if q == 0 else jnp.where(used, factor, 0.0)

    def back_right(q, k):
        ys = []
        for b in range(2):
            factor = power[q, b]
            g = jnp.concatenate([far[q, k, b, :, :half] * factor, far[q, k, b, :, half:] * factor], 1)
            ys.append(dot(g.astype(BF16), mats[0, b]))
        for side, y in enumerate((ys[0] + ys[1], ys[0] - ys[1])):
            y = y.astype(BF16)
            cols = slice(side * half, (side + 1) * half)
            for a in range(2):
                rows = slice(a * half, (a + 1) * half)
                across[q, k, a, :half, cols] = y[rows, :half]
                across[q, k, a, half:, cols] = y[rows, half:]

    def back_left(k):
        vs = [(dot(mats[1, 0], across[q, k, 0]), dot(mats[1, 1], across[q, k, 1])) for q in range(PAIR)]
        for side in range(2):
            rows = slice(side * half, (side + 1) * half)
            pr, pi = probe[k, 0, rows, :], probe[k, 1, rows, :]
            sum_re, sum_im = probe_sum[rows_of(k, 0, rows), :], probe_sum[rows_of(k, 1, rows), :]
            for q, (v0, v1) in enumerate(vs):
                v = v0 + v1 if side == 0 else v0 - v1
                g_re, g_im = v[:half], v[half:]
                o_re, o_im = window[q, 0, rows, :], window[q, 1, rows, :]
                add_re = pr * g_re + pi * g_im
                add_im = pr * g_im - pi * g_re
                part[q, 0, rows, :] = add_re if k == 0 else part[q, 0, rows, :] + add_re
                part[q, 1, rows, :] = add_im if k == 0 else part[q, 1, rows, :] + add_im
                sum_re = sum_re + o_re * g_re + o_im * g_im
                sum_im = sum_im + o_re * g_im - o_im * g_re
            probe_sum[rows_of(k, 0, rows), :] = sum_re
            probe_sum[rows_of(k, 1, rows), :] = sum_im

    @pl.loop(0, (count + PAIR - 1) // PAIR)
    def _(step):
        numbers = [jnp.minimum(step * PAIR + q, count - 1) for q in range(PAIR)]
        amp_loads = [pltpu.make_async_copy(amps.at[n], amp.at[q], amp_sems.at[q]) for q, n in enumerate(numbers)]
        for load in amp_loads:
            load.start()
        places = []
        for q, n in enumerate(numbers):
            col_at = lax.rem(offsets[n, 1], tile_cols)
            places.append((lax.rem(offsets[n, 0], tile_rows), col_at // LANES, lax.rem(col_at, LANES)))
            take(q, *places[q])
        every = [(q, k) for k in range(modes) for q in range(PAIR)]
        for k in range(modes):
            psi(k)
        for q, k in every:
            left(q, k)
        for q, k in every:
            right(q, k)
        for load in amp_loads:
            load.wait()
        for q in range(PAIR):
            factors(q, step * PAIR + q < count)
        for q, k in every:
            back_right(q, k)
        for k in range(modes):
            back_left(k)
        for q in range(PAIR):
            give(q, *places[q])

    own_half = (lax.axis_index("narrow") & 1) * (probe_sum.shape[0] // 2)
    other_half = probe_sum.shape[0] // 2 - own_half
    pairs = [
        (probe_sum.at[pl.ds(pl.multiple_of(start, 8), probe_sum.shape[0] // 2), :], dst)
        for start, dst in ((other_half, probe_send), (own_half, probe_keep))
    ]
    for array, rows, cols in (
        (grad_corner, low_rows, rim),
        (grad_below, low_rows, whole),
        (grad_right, slice(0, extent), rim),
        (grad_right_low, slice(extent, tile_rows), rim),
        (grad_own, slice(0, tile_rows), whole),
    ):
        pairs += [(grad.at[at], dst) for dst, at in strips(array, rows, cols)]
    stores = [pltpu.make_async_copy(src, dst, out_sems.at[n]) for n, (src, dst) in enumerate(pairs)]
    for store in stores:
        store.start()
    for store in stores:
        store.wait()


def run_slots(offsets, live, own, below, right, right_low, corner, probe, amps):
    extent = probe.shape[2]
    modes = probe.shape[0]
    tile_rows, tile_cols = own.shape[1:]
    mats = jnp.asarray(half_dft(extent))
    order = jnp.asarray(parity_order(extent)).astype(BF16)
    smem = pl.BlockSpec(memory_space=pltpu.SMEM)
    vmem = pl.BlockSpec(memory_space=pltpu.VMEM)
    hbm = pl.BlockSpec(memory_space=pltpu.HBM)
    anywhere = pl.BlockSpec(memory_space=pl.ANY)
    tiles_shape = (2, (tile_cols + extent) // LANES, tile_rows + extent, LANES)
    sum_shape = (modes * 2 * extent, extent)
    half_sum = (sum_shape[0] // 2, extent)
    outs = [(2, tile_rows, tile_cols), (2, extent, tile_cols), (2, extent, extent), (2, tile_rows - extent, extent)]
    outs += [(2, extent, extent), half_sum, half_sum]
    return pl.pallas_call(
        functools.partial(slots_kernel, tile_rows, tile_cols),
        out_shape=[jax.ShapeDtypeStruct(shape, F32) for shape in outs],
        in_specs=[smem, smem, hbm] + [anywhere] * 4 + [hbm, hbm, vmem, vmem],
        out_specs=[anywhere] * len(outs),
        scratch_shapes=[
            pltpu.VMEM(tiles_shape, F32),
            pltpu.VMEM(tiles_shape, F32),
            pltpu.VMEM(probe.shape, F32),
            pltpu.VMEM(sum_shape, F32),
            pltpu.VMEM((PAIR, 2, extent, extent), F32),
            pltpu.VMEM((PAIR, 2, extent, extent), F32),
            pltpu.VMEM((PAIR, extent, extent), F32),
            pltpu.VMEM((PAIR, 2, extent, extent // 2), F32),
            pltpu.VMEM((PAIR, modes, 2, extent, extent), BF16),
            pltpu.VMEM((PAIR, modes, 2, extent, extent), BF16),
            pltpu.VMEM((PAIR, modes, 2, extent, extent), F32),
            pltpu.VMEM((PAIR, 2, extent, extent // 2), F32),
            pltpu.VMEM((PAIR, modes, 2, extent, extent), BF16),
            pltpu.SemaphoreType.DMA((4 * tiles_shape[1],)),
            pltpu.SemaphoreType.DMA((PAIR,)),
            pltpu.SemaphoreType.DMA((4 * tiles_shape[1],)),
        ],
        compiler_params=pltpu.CompilerParams(vmem_limit_bytes=44 * 1024 * 1024),
        name="slots",
    )(offsets, live, own, below, right, right_low, corner, probe, amps, mats, order)


def shifted(value, axis, steps):
    count = lax.axis_size(axis)
    first, last = (max(0, -steps), min(count, count - steps))
    return lax.ppermute(value, axis, [(source, source + steps) for source in range(first, last)])


def place_in(bits):
    linear = lax.axis_index("wide") * lax.axis_size("narrow") + lax.axis_index("narrow")
    place = 0
    for n, bit in enumerate(bits):
        place = place + ((linear // bit) % 2) * (1 << n)
    return place


def partners(bits):
    return [sum(bit for n, bit in enumerate(bits) if step >> n & 1) for step in range(1 << len(bits))]


def swapped(value, mask):
    count = lax.axis_size("wide") * lax.axis_size("narrow")
    return lax.ppermute(value, ("wide", "narrow"), [(source, source ^ mask) for source in range(count)])


def add_kernel(bits, count, *refs):
    ins, outs = refs[:count], refs[count:]
    rows = outs[0].shape[0]
    place = place_in(bits)
    for step, out in enumerate(outs):
        at = pl.ds(pl.multiple_of((place ^ step) * rows, 8), rows)
        out[...] = sum(ref[at, :] for ref in ins)


def add_parts(parts, bits):
    count = 1 << len(bits)
    rows, cols = parts[0].shape
    vmem = pl.BlockSpec(memory_space=pltpu.VMEM)
    return pl.pallas_call(
        functools.partial(add_kernel, bits, len(parts)),
        out_shape=[jax.ShapeDtypeStruct((rows // count, cols), F32)] * count,
        in_specs=[vmem] * len(parts),
        out_specs=[vmem] * count,
        compiler_params=pltpu.CompilerParams(vmem_limit_bytes=8 * 1024 * 1024),
        name="add_parts",
    )(*parts)


def join_kernel(bits, scale, *refs):
    ins, out = refs[:-1], refs[-1]
    rows = ins[0].shape[0]
    place = place_in(bits)
    for step, ref in enumerate(ins):
        at = pl.ds(pl.multiple_of((place ^ step) * rows, 8), rows)
        out[at, :] = ref[...] if scale is None else ref[...] * scale


def join_parts(parts, bits, scale=None):
    rows, cols = parts[0].shape
    vmem = pl.BlockSpec(memory_space=pltpu.VMEM)
    return pl.pallas_call(
        functools.partial(join_kernel, bits, scale),
        out_shape=jax.ShapeDtypeStruct((rows * len(parts), cols), F32),
        in_specs=[vmem] * len(parts),
        out_specs=vmem,
        compiler_params=pltpu.CompilerParams(vmem_limit_bytes=8 * 1024 * 1024),
        name="join_parts",
    )(*parts)


def together(*values):
    return lax.optimization_barrier(values)


def sum_everywhere(keep, send, scale, grad_right, came_right_low, grad_below):
    narrow, wide = lax.axis_size("narrow"), lax.axis_size("wide")
    bits = [1 << n for n in range((narrow * wide).bit_length() - 1)]
    rest = bits[1:]
    groups = [tuple(rest[n :: (len(rest) + 1) // 2]) for n in range((len(rest) + 1) // 2)]
    parts = [keep, swapped(send, bits[0])]
    for n, group in enumerate(groups):
        pieces = add_parts(parts, group)
        if n == 0:
            pieces, grad_right = together(pieces, grad_right)
            came_right = shifted(grad_right, "wide", 1)
        if n == 1:
            pieces, grad_below = together(pieces, grad_below)
            came_below = shifted(grad_below, "narrow", 1)
        parts = [pieces[0]] + [swapped(piece, mask) for piece, mask in zip(pieces[1:], partners(group)[1:])]
        if n == 0:
            parts, came_right_low = together(parts, came_right_low)
    value = add_parts(parts, ())[0]
    for group in reversed(groups):
        if group == groups[0]:
            value, came_right, came_below = together(value, came_right, came_below)
        parts = [value] + [swapped(value, mask) for mask in partners(group)[1:]]
        if group != groups[0]:
            value = join_parts(parts, group)
    parts = parts + [swapped(part, bits[0]) for part in parts]
    return join_parts(parts, groups[0] + (bits[0],), scale), came_right, came_right_low, came_below


def on_device(object_field, probe, amplitudes, offsets, live):
    extent = probe.shape[2]
    top, whole = together(object_field[:, :extent], object_field)
    right = shifted(top, "wide", -1)
    below = shifted(top, "narrow", -1)
    right_low = shifted(whole[:, extent:], "wide", -1)
    corner = shifted(right, "narrow", -1)
    grad_own, grad_below, grad_right, grad_right_low, grad_corner, keep, send = run_slots(
        offsets, live, object_field, below, right, right_low, corner, probe, amplitudes
    )
    came_right_low = shifted(grad_right_low, "wide", 1)
    grad_right = grad_right + shifted(grad_corner, "narrow", 1)
    total_slots = lax.axis_size("wide") * lax.axis_size("narrow") * offsets.shape[0]
    probe_grad, came_right, came_right_low, came_below = sum_everywhere(
        keep, send, 1.0 / math.sqrt(total_slots), grad_right, came_right_low, grad_below
    )
    rims = jnp.concatenate([came_right, came_right_low], 1)
    object_grad = grad_own.at[:, :extent, :].add(came_below).at[:, :, :extent].add(rims)
    return (object_grad, probe_grad.reshape(probe.shape))


def solution(mesh):
    return jax.shard_map(
        on_device,
        mesh=mesh,
        in_specs=(
            P(None, "narrow", "wide"),
            P(),
            P(("wide", "narrow"), None, None),
            P(("wide", "narrow"), None),
            P(("wide", "narrow")),
        ),
        out_specs=(P(None, "narrow", "wide"), P()),
        check_vma=False,
    )
```

profile of v0, /device:TPU:0, one launch (start us, length us, event | category | flops | bytes accessed | tf_op | source)
XLA Modules:
  0.0 122.7 jit_solution(17118358484643340161)
XLA Ops:
  0.7 2.0 %slice.49 = f32[2,256,256]{2,1,0:T(8,128)} slice(f32[2,512,256]{2,1,0:T(8,128)} %own.1), slice={[0:2], [0:256], [0:256]} | slice | bytes 1048576 | tf_op jit(solution)/shard_map/slice | solution.py:380
  2.7 1.3 %collective-permute-start.1 = (f32[2,256,256]{2,1,0:T(8,128)}, f32[2,256,256]{2,1,0:T(8,128)S(1)}, u32[]{:S(2)}, u32[]{:S(2)}) collective-permute-start(f32[2,256,256]{2,1,0:T(8,128)} %slice.49), channel_id=1, source_target_pairs={{4,0},{8,4},{12,8},{16,12},{20,16},{24,20},{28,24},{5,1},{9,5},{13... | collective-permute-start | bytes 1572872 | tf_op jit(solution)/shard_map/ppermute | solution.py:281
  4.0 1.3 %collective-permute-start = (f32[2,256,256]{2,1,0:T(8,128)}, f32[2,256,256]{2,1,0:T(8,128)S(1)}, u32[]{:S(2)}, u32[]{:S(2)}) collective-permute-start(f32[2,256,256]{2,1,0:T(8,128)} %slice.49), channel_id=1, source_target_pairs={{1,0},{2,1},{3,2},{5,4},{6,5},{7,6},{9,8},{10,9},{11,10},{13,12},{... | collective-permute-start | bytes 1572872 | tf_op jit(solution)/shard_map/ppermute | solution.py:281
  5.3 1.9 %slice.50 = f32[2,256,256]{2,1,0:T(8,128)} slice(f32[2,512,256]{2,1,0:T(8,128)} %own.1), slice={[0:2], [256:512], [0:256]} | slice | bytes 1048576 | tf_op jit(solution)/shard_map/slice | solution.py:383
  7.1 1.3 %collective-permute-start.2 = (f32[2,256,256]{2,1,0:T(8,128)}, f32[2,256,256]{2,1,0:T(8,128)S(1)}, u32[]{:S(2)}, u32[]{:S(2)}) collective-permute-start(f32[2,256,256]{2,1,0:T(8,128)} %slice.50), channel_id=1, source_target_pairs={{4,0},{8,4},{12,8},{16,12},{20,16},{24,20},{28,24},{5,1},{9,5},{13... | collective-permute-start | bytes 1572872 | tf_op jit(solution)/shard_map/ppermute | solution.py:281
  8.4 12.0 %collective-permute-done.1.right = f32[2,256,256]{2,1,0:T(8,128)S(1)} collective-permute-done((f32[2,256,256]{2,1,0:T(8,128)}, f32[2,256,256]{2,1,0:T(8,128)S(1)}, u32[]{:S(2)}, u32[]{:S(2)}) %collective-permute-start.1) | collective-permute-done | bytes 524320 | tf_op jit(solution)/shard_map/ppermute | solution.py:281
  20.5 1.3 %collective-permute-start.3 = (f32[2,256,256]{2,1,0:T(8,128)S(1)}, f32[2,256,256]{2,1,0:T(8,128)}, u32[]{:S(2)}, u32[]{:S(2)}) collective-permute-start(f32[2,256,256]{2,1,0:T(8,128)S(1)} %collective-permute-done.1.right), channel_id=1, source_target_pairs={{1,0},{2,1},{3,2},{5,4},{6,5},{7,6},{9,8},{10,9},{11,10},{13,12},{... | collective-permute-start | bytes 1572872 | tf_op jit(solution)/shard_map/ppermute | solution.py:281
  22.5 8.4 %collective-permute-done.2.right_low = f32[2,256,256]{2,1,0:T(8,128)S(1)} collective-permute-done((f32[2,256,256]{2,1,0:T(8,128)}, f32[2,256,256]{2,1,0:T(8,128)S(1)}, u32[]{:S(2)}, u32[]{:S(2)}) %collective-permute-start.2) | collective-permute-done | bytes 524320 | tf_op jit(solution)/shard_map/ppermute | solution.py:281
  30.9 13.8 %slots.1 = (f32[2,512,256]{2,1,0:T(8,128)S(1)}, f32[2,256,256]{2,1,0:T(8,128)S(1)}, f32[2,256,256]{2,1,0:T(8,128)S(1)}, f32[2,256,256]{2,1,0:T(8,128)S(1)}, f32[...) custom-call(s32[8,2]{1,0:T(8,128)S(1)} %copy.9.offsets, s32[1]{0:T(128)S(6)} %copy.11.live, ...), custom_call_target="tpu_custom_call" | custom-call | tf_op jit(solution)/shard_map/slots/pallas_call | solution.py:250
  44.8 2.4 %collective-permute-start.5 = (f32[2,256,256]{2,1,0:T(8,128)S(1)}, f32[2,256,256]{2,1,0:T(8,128)S(1)}, u32[]{:S(2)}, u32[]{:S(2)}) collective-permute-start(f32[2,256,256]{2,1,0:T(8,128)S(1)} %get-tuple-element.79), channel_id=1, source_target_pairs={{0,1},{1,2},{2,3},{4,5},{5,6},{6,7},{8,9},{9,10},{10,11},{12,13},{... | collective-permute-start | bytes 1572872 | tf_op jit(solution)/shard_map/ppermute | solution.py:281
  47.2 4.6 %collective-permute-start.9 = (f32[2,256,256]{2,1,0:T(8,128)S(1)}, f32[2,256,256]{2,1,0:T(8,128)S(1)}, u32[]{:S(2)}, u32[]{:S(2)}) collective-permute-start(f32[2,256,256]{2,1,0:T(8,128)S(1)} %get-tuple-element.84), channel_id=1, source_target_pairs={{0,4},{4,8},{8,12},{12,16},{16,20},{20,24},{24,28},{1,5},{5,9},{9,... | collective-permute-start | bytes 1572872 | tf_op jit(solution)/shard_map/ppermute | solution.py:281
  52.0 5.3 %collective-permute-start.6 = (f32[256,256]{1,0:T(8,128)S(1)}, f32[256,256]{1,0:T(8,128)S(1)}, u32[]{:S(2)}, u32[]{:S(2)}) collective-permute-start(f32[256,256]{1,0:T(8,128)S(1)} %get-tuple-element.81), channel_id=1, source_target_pairs={{0,2},{1,3},{2,0},{3,1},{4,6},{5,7},{6,4},{7,5},{8,10},{9,11},{10,... | collective-permute-start | bytes 786440 | tf_op jit(solution)/shard_map/ppermute | solution.py:298
  57.3 8.3 %collective-permute-start.7 = (f32[256,256]{1,0:T(8,128)S(1)}, f32[256,256]{1,0:T(8,128)S(1)}, u32[]{:S(2)}, u32[]{:S(2)}) collective-permute-start(f32[256,256]{1,0:T(8,128)S(1)} %get-tuple-element.82), channel_id=1, source_target_pairs={{0,8},{1,9},{2,10},{3,11},{4,12},{5,13},{6,14},{7,15},{8,0},{9,1},... | collective-permute-start | bytes 786440 | tf_op jit(solution)/shard_map/ppermute | solution.py:298
  65.6 8.1 %collective-permute-start.16 = (f32[2,256,256]{2,1,0:T(8,128)S(1)}, f32[2,256,256]{2,1,0:T(8,128)S(1)}, u32[]{:S(2)}, u32[]{:S(2)}) collective-permute-start(f32[2,256,256]{2,1,0:T(8,128)S(1)} %add.19), channel_id=1, source_target_pairs={{0,4},{4,8},{8,12},{12,16},{16,20},{20,24},{24,28},{1,5},{5,9},{9,... | collective-permute-start | bytes 1572872 | tf_op jit(solution)/shard_map/ppermute | solution.py:281
  73.7 3.8 %collective-permute-done.8.refs_3_ = f32[256,256]{1,0:T(8,128)S(1)} collective-permute-done((f32[256,256]{1,0:T(8,128)S(1)}, f32[256,256]{1,0:T(8,128)S(1)}, u32[]{:S(2)}, u32[]{:S(2)}) %collective-permute-start.8) | collective-permute-done | bytes 262176 | tf_op jit(solution)/shard_map/ppermute | solution.py:298
  77.6 2.1 %collective-permute-start.17 = (f32[2,256,256]{2,1,0:T(8,128)S(1)}, f32[2,256,256]{2,1,0:T(8,128)S(1)}, u32[]{:S(2)}, u32[]{:S(2)}) collective-permute-start(f32[2,256,256]{2,1,0:T(8,128)S(1)} %get-tuple-element.99), channel_id=1, source_target_pairs={{0,1},{1,2},{2,3},{4,5},{5,6},{6,7},{8,9},{9,10},{10,11},{12,13},{... | collective-permute-start | bytes 1572872 | tf_op jit(solution)/shard_map/ppermute | solution.py:281
  79.7 5.9 %collective-permute-start.10 = (f32[64,256]{1,0:T(8,128)S(1)}, f32[64,256]{1,0:T(8,128)S(1)}, u32[]{:S(2)}, u32[]{:S(2)}) collective-permute-start(f32[64,256]{1,0:T(8,128)S(1)} %get-tuple-element.95), channel_id=1, source_target_pairs={{0,4},{1,5},{2,6},{3,7},{4,0},{5,1},{6,2},{7,3},{8,12},{9,13},{10,... | collective-permute-start | bytes 196616 | tf_op jit(solution)/shard_map/ppermute | solution.py:298
  85.6 2.4 %collective-permute-start.12 = (f32[64,256]{1,0:T(8,128)S(1)}, f32[64,256]{1,0:T(8,128)S(1)}, u32[]{:S(2)}, u32[]{:S(2)}) collective-permute-start(f32[64,256]{1,0:T(8,128)S(1)} %get-tuple-element.97), channel_id=1, source_target_pairs={{0,20},{1,21},{2,22},{3,23},{4,16},{5,17},{6,18},{7,19},{8,28},{9,... | collective-permute-start | bytes 196616 | tf_op jit(solution)/shard_map/ppermute | solution.py:298
  88.5 2.9 %collective-permute-done.11.refs_2_ = f32[64,256]{1,0:T(8,128)S(1)} collective-permute-done((f32[64,256]{1,0:T(8,128)S(1)}, f32[64,256]{1,0:T(8,128)S(1)}, u32[]{:S(2)}, u32[]{:S(2)}) %collective-permute-start.11) | collective-permute-done | bytes 65568 | tf_op jit(solution)/shard_map/ppermute | solution.py:298
  91.4 3.6 %collective-permute-done.12.refs_3_ = f32[64,256]{1,0:T(8,128)S(1)} collective-permute-done((f32[64,256]{1,0:T(8,128)S(1)}, f32[64,256]{1,0:T(8,128)S(1)}, u32[]{:S(2)}, u32[]{:S(2)}) %collective-permute-start.12) | collective-permute-done | bytes 65568 | tf_op jit(solution)/shard_map/ppermute | solution.py:298
  95.0 2.4 %collective-permute-start.15 = (f32[64,256]{1,0:T(8,128)S(1)}, f32[64,256]{1,0:T(8,128)S(1)}, u32[]{:S(2)}, u32[]{:S(2)}) collective-permute-start(f32[64,256]{1,0:T(8,128)S(1)} %add_parts.5.refs_0_), channel_id=1, source_target_pairs={{0,20},{1,21},{2,22},{3,23},{4,16},{5,17},{6,18},{7,19},{8,28},{9,... | collective-permute-start | bytes 196616 | tf_op jit(solution)/shard_map/ppermute | solution.py:298
  97.4 1.7 %collective-permute-start.14 = (f32[64,256]{1,0:T(8,128)S(1)}, f32[64,256]{1,0:T(8,128)S(1)}, u32[]{:S(2)}, u32[]{:S(2)}) collective-permute-start(f32[64,256]{1,0:T(8,128)S(1)} %add_parts.5.refs_0_), channel_id=1, source_target_pairs={{0,16},{1,17},{2,18},{3,19},{4,20},{5,21},{6,22},{7,23},{8,24},{9,... | collective-permute-start | bytes 196616 | tf_op jit(solution)/shard_map/ppermute | solution.py:298
  99.1 0.4 collective-permute-start.13
  99.6 4.8 %collective-permute-done.15.refs_3_ = f32[64,256]{1,0:T(8,128)S(1)} collective-permute-done((f32[64,256]{1,0:T(8,128)S(1)}, f32[64,256]{1,0:T(8,128)S(1)}, u32[]{:S(2)}, u32[]{:S(2)}) %collective-permute-start.15) | collective-permute-done | bytes 65568 | tf_op jit(solution)/shard_map/ppermute | solution.py:298
  104.5 1.7 %collective-permute-start.20 = (f32[256,256]{1,0:T(8,128)S(1)}, f32[256,256]{1,0:T(8,128)S(1)}, u32[]{:S(2)}, u32[]{:S(2)}) collective-permute-start(f32[256,256]{1,0:T(8,128)S(1)} %join_parts.2.refs_0_), channel_id=1, source_target_pairs={{0,10},{1,11},{2,8},{3,9},{4,14},{5,15},{6,12},{7,13},{8,2},{9,3},... | collective-permute-start | bytes 786440 | tf_op jit(solution)/shard_map/ppermute | solution.py:298
  106.1 0.8 collective-permute-start.19
  106.9 1.1 collective-permute-start.18
  108.2 6.4 %collective-permute-done.20.refs_3_ = f32[256,256]{1,0:T(8,128)S(1)} collective-permute-done((f32[256,256]{1,0:T(8,128)S(1)}, f32[256,256]{1,0:T(8,128)S(1)}, u32[]{:S(2)}, u32[]{:S(2)}) %collective-permute-start.20) | collective-permute-done | bytes 262176 | tf_op jit(solution)/shard_map/ppermute | solution.py:298
  114.6 4.6 %collective-permute-done.19.refs_2_ = f32[256,256]{1,0:T(8,128)S(1)} collective-permute-done((f32[256,256]{1,0:T(8,128)S(1)}, f32[256,256]{1,0:T(8,128)S(1)}, u32[]{:S(2)}, u32[]{:S(2)}) %collective-permute-start.19) | collective-permute-done | bytes 262176 | tf_op jit(solution)/shard_map/ppermute | solution.py:298
  119.2 0.5 collective-permute-done.18.refs_1_
  119.7 1.1 maximum_add_fusion
  121.3 1.5 %join_parts.3 = f32[2048,256]{1,0:T(8,128)} custom-call(f32[256,256]{1,0:T(8,128)S(1)} %join_parts.2.refs_0_, f32[256,256]{1,0:T(8,128)S(1)} %collective-permute-done.18.refs_1_, f32[256,256]{1,0:T(8,128)S(1)} %collective-permute-done.19.refs_2_, f32[256,256]{1,0:T(8,128)S(1)} %collective-permute-done.20.refs_3_, ...), custom_call_target="tpu_custom_call" | custom-call | tf_op jit(solution)/shard_map/join_parts/pallas_call | solution.py:336
  (38 shorter events, 1.6 us)
Async XLA Ops:
  0.6 30.2 %copy-start.2 = (bf16[256,256]{1,0:T(8,128)(2,1)S(1)}, bf16[256,256]{1,0:T(8,128)(2,1)}, u32[]{:S(2)}) copy-start(bf16[256,256]{1,0:T(8,128)(2,1)} %constant.71.order) | copy-start | bytes 393220
  0.6 30.2 %copy-start.1 = (bf16[2,2,256,256]{3,2,1,0:T(8,128)(2,1)S(1)}, bf16[2,2,256,256]{3,2,1,0:T(8,128)(2,1)}, u32[]{:S(2)}) copy-start(bf16[2,2,256,256]{3,2,1,0:T(8,128)(2,1)} %constant.66.clone.mats) | copy-start | bytes 1572868
  0.7 30.2 %copy-start = (f32[2,512,256]{2,1,0:T(8,128)S(1)}, f32[2,512,256]{2,1,0:T(8,128)}, u32[]{:S(2)}) copy-start(f32[2,512,256]{2,1,0:T(8,128)} %own.1) | copy-start | bytes 3145732
  0.7 21.7 %copy-start.3 = (s32[8,2]{0,1:T(2,128)S(1)}, s32[8,2]{0,1:T(2,128)}, u32[]{:S(2)}) copy-start(s32[8,2]{0,1:T(2,128)} %param.16) | copy-start | bytes 196
  2.7 17.8 %collective-permute-start.1 = (f32[2,256,256]{2,1,0:T(8,128)}, f32[2,256,256]{2,1,0:T(8,128)S(1)}, u32[]{:S(2)}, u32[]{:S(2)}) collective-permute-start(f32[2,256,256]{2,1,0:T(8,128)} %slice.49), channel_id=1, source_target_pairs={{4,0},{8,4},{12,8},{16,12},{20,16},{24,20},{28,24},{5,1},{9,5},{13... | collective-permute-start | bytes 1572872 | tf_op jit(solution)/shard_map/ppermute | solution.py:281
  4.0 26.9 %collective-permute-start = (f32[2,256,256]{2,1,0:T(8,128)}, f32[2,256,256]{2,1,0:T(8,128)S(1)}, u32[]{:S(2)}, u32[]{:S(2)}) collective-permute-start(f32[2,256,256]{2,1,0:T(8,128)} %slice.49), channel_id=1, source_target_pairs={{1,0},{2,1},{3,2},{5,4},{6,5},{7,6},{9,8},{10,9},{11,10},{13,12},{... | collective-permute-start | bytes 1572872 | tf_op jit(solution)/shard_map/ppermute | solution.py:281
  7.1 23.7 %collective-permute-start.2 = (f32[2,256,256]{2,1,0:T(8,128)}, f32[2,256,256]{2,1,0:T(8,128)S(1)}, u32[]{:S(2)}, u32[]{:S(2)}) collective-permute-start(f32[2,256,256]{2,1,0:T(8,128)} %slice.50), channel_id=1, source_target_pairs={{4,0},{8,4},{12,8},{16,12},{20,16},{24,20},{28,24},{5,1},{9,5},{13... | collective-permute-start | bytes 1572872 | tf_op jit(solution)/shard_map/ppermute | solution.py:281
  20.5 10.4 %collective-permute-start.3 = (f32[2,256,256]{2,1,0:T(8,128)S(1)}, f32[2,256,256]{2,1,0:T(8,128)}, u32[]{:S(2)}, u32[]{:S(2)}) collective-permute-start(f32[2,256,256]{2,1,0:T(8,128)S(1)} %collective-permute-done.1.right), channel_id=1, source_target_pairs={{1,0},{2,1},{3,2},{5,4},{6,5},{7,6},{9,8},{10,9},{11,10},{13,12},{... | collective-permute-start | bytes 1572872 | tf_op jit(solution)/shard_map/ppermute | solution.py:281
  44.7 7.2 %collective-permute-start.4 = (f32[1024,256]{1,0:T(8,128)S(1)}, f32[1024,256]{1,0:T(8,128)S(1)}, u32[]{:S(2)}, u32[]{:S(2)}) collective-permute-start(f32[1024,256]{1,0:T(8,128)S(1)} %get-tuple-element.73), channel_id=1, source_target_pairs={{0,1},{1,0},{2,3},{3,2},{4,5},{5,4},{6,7},{7,6},{8,9},{9,8},{10,11... | collective-permute-start | bytes 3145736 | tf_op jit(solution)/shard_map/ppermute | solution.py:298
  44.8 7.0 %collective-permute-start.5 = (f32[2,256,256]{2,1,0:T(8,128)S(1)}, f32[2,256,256]{2,1,0:T(8,128)S(1)}, u32[]{:S(2)}, u32[]{:S(2)}) collective-permute-start(f32[2,256,256]{2,1,0:T(8,128)S(1)} %get-tuple-element.79), channel_id=1, source_target_pairs={{0,1},{1,2},{2,3},{4,5},{5,6},{6,7},{8,9},{9,10},{10,11},{12,13},{... | collective-permute-start | bytes 1572872 | tf_op jit(solution)/shard_map/ppermute | solution.py:281
  47.2 26.5 %collective-permute-start.9 = (f32[2,256,256]{2,1,0:T(8,128)S(1)}, f32[2,256,256]{2,1,0:T(8,128)S(1)}, u32[]{:S(2)}, u32[]{:S(2)}) collective-permute-start(f32[2,256,256]{2,1,0:T(8,128)S(1)} %get-tuple-element.84), channel_id=1, source_target_pairs={{0,4},{4,8},{8,12},{12,16},{16,20},{20,24},{24,28},{1,5},{5,9},{9,... | collective-permute-start | bytes 1572872 | tf_op jit(solution)/shard_map/ppermute | solution.py:281
  52.0 21.7 %collective-permute-start.6 = (f32[256,256]{1,0:T(8,128)S(1)}, f32[256,256]{1,0:T(8,128)S(1)}, u32[]{:S(2)}, u32[]{:S(2)}) collective-permute-start(f32[256,256]{1,0:T(8,128)S(1)} %get-tuple-element.81), channel_id=1, source_target_pairs={{0,2},{1,3},{2,0},{3,1},{4,6},{5,7},{6,4},{7,5},{8,10},{9,11},{10,... | collective-permute-start | bytes 786440 | tf_op jit(solution)/shard_map/ppermute | solution.py:298
  57.3 16.4 %collective-permute-start.7 = (f32[256,256]{1,0:T(8,128)S(1)}, f32[256,256]{1,0:T(8,128)S(1)}, u32[]{:S(2)}, u32[]{:S(2)}) collective-permute-start(f32[256,256]{1,0:T(8,128)S(1)} %get-tuple-element.82), channel_id=1, source_target_pairs={{0,8},{1,9},{2,10},{3,11},{4,12},{5,13},{6,14},{7,15},{8,0},{9,1},... | collective-permute-start | bytes 786440 | tf_op jit(solution)/shard_map/ppermute | solution.py:298
  65.6 12.0 %collective-permute-start.8 = (f32[256,256]{1,0:T(8,128)S(1)}, f32[256,256]{1,0:T(8,128)S(1)}, u32[]{:S(2)}, u32[]{:S(2)}) collective-permute-start(f32[256,256]{1,0:T(8,128)S(1)} %get-tuple-element.83), channel_id=1, source_target_pairs={{0,10},{1,11},{2,8},{3,9},{4,14},{5,15},{6,12},{7,13},{8,2},{9,3},... | collective-permute-start | bytes 786440 | tf_op jit(solution)/shard_map/ppermute | solution.py:298
  65.6 38.8 %collective-permute-start.16 = (f32[2,256,256]{2,1,0:T(8,128)S(1)}, f32[2,256,256]{2,1,0:T(8,128)S(1)}, u32[]{:S(2)}, u32[]{:S(2)}) collective-permute-start(f32[2,256,256]{2,1,0:T(8,128)S(1)} %add.19), channel_id=1, source_target_pairs={{0,4},{4,8},{8,12},{12,16},{16,20},{20,24},{24,28},{1,5},{5,9},{9,... | collective-permute-start | bytes 1572872 | tf_op jit(solution)/shard_map/ppermute | solution.py:281
  77.6 26.8 %collective-permute-start.17 = (f32[2,256,256]{2,1,0:T(8,128)S(1)}, f32[2,256,256]{2,1,0:T(8,128)S(1)}, u32[]{:S(2)}, u32[]{:S(2)}) collective-permute-start(f32[2,256,256]{2,1,0:T(8,128)S(1)} %get-tuple-element.99), channel_id=1, source_target_pairs={{0,1},{1,2},{2,3},{4,5},{5,6},{6,7},{8,9},{9,10},{10,11},{12,13},{... | collective-permute-start | bytes 1572872 | tf_op jit(solution)/shard_map/ppermute | solution.py:281
  79.7 8.7 %collective-permute-start.10 = (f32[64,256]{1,0:T(8,128)S(1)}, f32[64,256]{1,0:T(8,128)S(1)}, u32[]{:S(2)}, u32[]{:S(2)}) collective-permute-start(f32[64,256]{1,0:T(8,128)S(1)} %get-tuple-element.95), channel_id=1, source_target_pairs={{0,4},{1,5},{2,6},{3,7},{4,0},{5,1},{6,2},{7,3},{8,12},{9,13},{10,... | collective-permute-start | bytes 196616 | tf_op jit(solution)/shard_map/ppermute | solution.py:298
  85.6 5.8 %collective-permute-start.11 = (f32[64,256]{1,0:T(8,128)S(1)}, f32[64,256]{1,0:T(8,128)S(1)}, u32[]{:S(2)}, u32[]{:S(2)}) collective-permute-start(f32[64,256]{1,0:T(8,128)S(1)} %get-tuple-element.96), channel_id=1, source_target_pairs={{0,16},{1,17},{2,18},{3,19},{4,20},{5,21},{6,22},{7,23},{8,24},{9,... | collective-permute-start | bytes 196616 | tf_op jit(solution)/shard_map/ppermute | solution.py:298
  85.6 9.4 %collective-permute-start.12 = (f32[64,256]{1,0:T(8,128)S(1)}, f32[64,256]{1,0:T(8,128)S(1)}, u32[]{:S(2)}, u32[]{:S(2)}) collective-permute-start(f32[64,256]{1,0:T(8,128)S(1)} %get-tuple-element.97), channel_id=1, source_target_pairs={{0,20},{1,21},{2,22},{3,23},{4,16},{5,17},{6,18},{7,19},{8,28},{9,... | collective-permute-start | bytes 196616 | tf_op jit(solution)/shard_map/ppermute | solution.py:298
  95.0 9.3 %collective-permute-start.15 = (f32[64,256]{1,0:T(8,128)S(1)}, f32[64,256]{1,0:T(8,128)S(1)}, u32[]{:S(2)}, u32[]{:S(2)}) collective-permute-start(f32[64,256]{1,0:T(8,128)S(1)} %add_parts.5.refs_0_), channel_id=1, source_target_pairs={{0,20},{1,21},{2,22},{3,23},{4,16},{5,17},{6,18},{7,19},{8,28},{9,... | collective-permute-start | bytes 196616 | tf_op jit(solution)/shard_map/ppermute | solution.py:298
  97.4 6.9 %collective-permute-start.14 = (f32[64,256]{1,0:T(8,128)S(1)}, f32[64,256]{1,0:T(8,128)S(1)}, u32[]{:S(2)}, u32[]{:S(2)}) collective-permute-start(f32[64,256]{1,0:T(8,128)S(1)} %add_parts.5.refs_0_), channel_id=1, source_target_pairs={{0,16},{1,17},{2,18},{3,19},{4,20},{5,21},{6,22},{7,23},{8,24},{9,... | collective-permute-start | bytes 196616 | tf_op jit(solution)/shard_map/ppermute | solution.py:298
  99.1 5.2 %collective-permute-start.13 = (f32[64,256]{1,0:T(8,128)S(1)}, f32[64,256]{1,0:T(8,128)S(1)}, u32[]{:S(2)}, u32[]{:S(2)}) collective-permute-start(f32[64,256]{1,0:T(8,128)S(1)} %add_parts.5.refs_0_), channel_id=1, source_target_pairs={{0,4},{1,5},{2,6},{3,7},{4,0},{5,1},{6,2},{7,3},{8,12},{9,13},{10,... | collective-permute-start | bytes 196616 | tf_op jit(solution)/shard_map/ppermute | solution.py:298
  104.4 16.4 %collective-permute-start.21 = (f32[256,256]{1,0:T(8,128)S(1)}, f32[256,256]{1,0:T(8,128)S(1)}, u32[]{:S(2)}, u32[]{:S(2)}) collective-permute-start(f32[256,256]{1,0:T(8,128)S(1)} %join_parts.2.refs_0_), channel_id=1, source_target_pairs={{0,1},{1,0},{2,3},{3,2},{4,5},{5,4},{6,7},{7,6},{8,9},{9,8},{10,11... | collective-permute-start | bytes 786440 | tf_op jit(solution)/shard_map/ppermute | solution.py:298
  104.5 10.1 %collective-permute-start.20 = (f32[256,256]{1,0:T(8,128)S(1)}, f32[256,256]{1,0:T(8,128)S(1)}, u32[]{:S(2)}, u32[]{:S(2)}) collective-permute-start(f32[256,256]{1,0:T(8,128)S(1)} %join_parts.2.refs_0_), channel_id=1, source_target_pairs={{0,10},{1,11},{2,8},{3,9},{4,14},{5,15},{6,12},{7,13},{8,2},{9,3},... | collective-permute-start | bytes 786440 | tf_op jit(solution)/shard_map/ppermute | solution.py:298
  106.1 13.1 %collective-permute-start.19 = (f32[256,256]{1,0:T(8,128)S(1)}, f32[256,256]{1,0:T(8,128)S(1)}, u32[]{:S(2)}, u32[]{:S(2)}) collective-permute-start(f32[256,256]{1,0:T(8,128)S(1)} %join_parts.2.refs_0_), channel_id=1, source_target_pairs={{0,8},{1,9},{2,10},{3,11},{4,12},{5,13},{6,14},{7,15},{8,0},{9,1},... | collective-permute-start | bytes 786440 | tf_op jit(solution)/shard_map/ppermute | solution.py:298
  106.9 12.8 %collective-permute-start.18 = (f32[256,256]{1,0:T(8,128)S(1)}, f32[256,256]{1,0:T(8,128)S(1)}, u32[]{:S(2)}, u32[]{:S(2)}) collective-permute-start(f32[256,256]{1,0:T(8,128)S(1)} %join_parts.2.refs_0_), channel_id=1, source_target_pairs={{0,2},{1,3},{2,0},{3,1},{4,6},{5,7},{6,4},{7,5},{8,10},{9,11},{10,... | collective-permute-start | bytes 786440 | tf_op jit(solution)/shard_map/ppermute | solution.py:298
  114.6 6.3 %collective-permute-start.24 = (f32[256,256]{1,0:T(8,128)S(1)}, f32[256,256]{1,0:T(8,128)S(1)}, u32[]{:S(2)}, u32[]{:S(2)}) collective-permute-start(f32[256,256]{1,0:T(8,128)S(1)} %collective-permute-done.20.refs_3_), channel_id=1, source_target_pairs={{0,1},{1,0},{2,3},{3,2},{4,5},{5,4},{6,7},{7,6},{8,9},{9,8},{10,11... | collective-permute-start | bytes 786440 | tf_op jit(solution)/shard_map/ppermute | solution.py:298
  119.2 1.6 %collective-permute-start.23 = (f32[256,256]{1,0:T(8,128)S(1)}, f32[256,256]{1,0:T(8,128)S(1)}, u32[]{:S(2)}, u32[]{:S(2)}) collective-permute-start(f32[256,256]{1,0:T(8,128)S(1)} %collective-permute-done.19.refs_2_), channel_id=1, source_target_pairs={{0,1},{1,0},{2,3},{3,2},{4,5},{5,4},{6,7},{7,6},{8,9},{9,8},{10,11... | collective-permute-start | bytes 786440 | tf_op jit(solution)/shard_map/ppermute | solution.py:298
  119.7 1.5 %collective-permute-start.22 = (f32[256,256]{1,0:T(8,128)S(1)}, f32[256,256]{1,0:T(8,128)S(1)}, u32[]{:S(2)}, u32[]{:S(2)}) collective-permute-start(f32[256,256]{1,0:T(8,128)S(1)} %collective-permute-done.18.refs_1_), channel_id=1, source_target_pairs={{0,1},{1,0},{2,3},{3,2},{4,5},{5,4},{6,7},{7,6},{8,9},{9,8},{10,11... | collective-permute-start | bytes 786440 | tf_op jit(solution)/shard_map/ppermute | solution.py:298
where the time goes:
time: 125 us; the launch traced here: 123 us
  starting transfers between devices  52.5 us (42%)
  waiting for transfers between devices  47.9 us (38%)
  Pallas kernels  15.5 us (12%)
  local copies, waits for them, and re-layouts  3.98 us (3%)
  between operations  1.53 us (1%)
  other arithmetic  1.3 us (1%)
    ppermute x17, starting transfers between devices, swapped(): lax.ppermute(value, ('wide', 'narrow'), [(source, source ^ mask) for sour...  30.2 us
    ppermute x17, waiting for transfers between devices, swapped(): lax.ppermute(value, ('wide', 'narrow'), [(source, source ^ mask) for sour...  27.5 us
    ppermute x8, starting transfers between devices, shifted(): lax.ppermute(value, axis, [(source, source + steps) for source in range(f...  22.3 us
    ppermute x8, waiting for transfers between devices, shifted(): lax.ppermute(value, axis, [(source, source + steps) for source in range(f...  20.4 us
    pallas_call x1, Pallas kernels, run_slots(): pl.pallas_call(functools.partial(slots_kernel, tile_rows, tile_cols), out...  13.8 us
  transfers between devices with their start and end apart: 25, of which 11 were waited for; matrix products, arithmetic and copies ran while one was open for 3% of the time, Pallas kernels for 0%

commit v1 on v0

--- a/solution.py
+++ b/solution.py
@@ -281,6 +281,12 @@
     return lax.ppermute(value, axis, [(source, source + steps) for source in range(first, last)])
 
 
+def aslant(value):
+    narrow, wide = lax.axis_size("narrow"), lax.axis_size("wide")
+    pairs = [(w * narrow + n, (w + 1) * narrow + n + 1) for w in range(wide - 1) for n in range(narrow - 1)]
+    return lax.ppermute(value, ("wide", "narrow"), pairs)
+
+
 def place_in(bits):
     linear = lax.axis_index("wide") * lax.axis_size("narrow") + lax.axis_index("narrow")
     place = 0
@@ -347,7 +353,7 @@
     return lax.optimization_barrier(values)
 
 
-def sum_everywhere(keep, send, scale, grad_right, came_right_low, grad_below):
+def sum_everywhere(keep, send, scale, grad_right, came_right_low, grad_corner, grad_below):
     narrow, wide = lax.axis_size("narrow"), lax.axis_size("wide")
     bits = [1 << n for n in range((narrow * wide).bit_length() - 1)]
     rest = bits[1:]
@@ -356,8 +362,9 @@
     for n, group in enumerate(groups):
         pieces = add_parts(parts, group)
         if n == 0:
-            pieces, grad_right = together(pieces, grad_right)
+            pieces, grad_right, grad_corner = together(pieces, grad_right, grad_corner)
             came_right = shifted(grad_right, "wide", 1)
+            came_corner = aslant(grad_corner)
         if n == 1:
             pieces, grad_below = together(pieces, grad_below)
             came_below = shifted(grad_below, "narrow", 1)
@@ -367,12 +374,12 @@
     value = add_parts(parts, ())[0]
     for group in reversed(groups):
         if group == groups[0]:
-            value, came_right, came_below = together(value, came_right, came_below)
+            value, came_right, came_corner, came_below = together(value, came_right, came_corner, came_below)
         parts = [value] + [swapped(value, mask) for mask in partners(group)[1:]]
         if group != groups[0]:
             value = join_parts(parts, group)
     parts = parts + [swapped(part, bits[0]) for part in parts]
-    return join_parts(parts, groups[0] + (bits[0],), scale), came_right, came_right_low, came_below
+    return join_parts(parts, groups[0] + (bits[0],), scale), came_right, came_right_low, came_corner, came_below
 
 
 def on_device(object_field, probe, amplitudes, offsets, live):
@@ -386,12 +393,11 @@
         offsets, live, object_field, below, right, right_low, corner, probe, amplitudes
     )
     came_right_low = shifted(grad_right_low, "wide", 1)
-    grad_right = grad_right + shifted(grad_corner, "narrow", 1)
     total_slots = lax.axis_size("wide") * lax.axis_size("narrow") * offsets.shape[0]
-    probe_grad, came_right, came_right_low, came_below = sum_everywhere(
-        keep, send, 1.0 / math.sqrt(total_slots), grad_right, came_right_low, grad_below
+    probe_grad, came_right, came_right_low, came_corner, came_below = sum_everywhere(
+        keep, send, 1.0 / math.sqrt(total_slots), grad_right, came_right_low, grad_corner, grad_below
     )
-    rims = jnp.concatenate([came_right, came_right_low], 1)
+    rims = jnp.concatenate([came_right + came_corner, came_right_low], 1)
     object_grad = grad_own.at[:, :extent, :].add(came_below).at[:, :, :extent].add(rims)
     return (object_grad, probe_grad.reshape(probe.shape))
 

time: 125 us -> 132 us (1.056); the launches traced: 123 us -> 131 us
  starting transfers between devices: 52.5 us -> 65.3 us
  Pallas kernels: 15.5 us -> 10.3 us
    ppermute x17, starting transfers between devices: 30.2 us -> 41.8 us  [swapped(): lax.ppermute(value, ('wide', 'narrow'), [(source, source ^ mask) for sour...]
    ppermute x8 -> x7, waiting for transfers between devices: 20.4 us -> 26.7 us  [shifted(): lax.ppermute(value, axis, [(source, source + steps) for source in range(f...]
    ppermute x17, waiting for transfers between devices: 27.5 us -> 22.1 us  [swapped(): lax.ppermute(value, ('wide', 'narrow'), [(source, source ^ mask) for sour...]
    pallas_call x1, Pallas kernels: 13.8 us -> 8.55 us  [run_slots(): pl.pallas_call(functools.partial(slots_kernel, tile_rows, tile_cols), out...]
    ppermute x0 -> x1, starting transfers between devices: none -> 2.26 us  [aslant(): return lax.ppermute(value, ('wide', 'narrow'), pairs)]
    ppermute x8 -> x7, starting transfers between devices: 22.3 us -> 21.2 us  [shifted(): lax.ppermute(value, axis, [(source, source + steps) for source in range(f...]
where the time goes in v1:
time: 132 us; the launch traced here: 131 us
  starting transfers between devices  65.3 us (49%)
  waiting for transfers between devices  48.9 us (37%)
  Pallas kernels  10.3 us (8%)
  local copies, waits for them, and re-layouts  3.98 us (3%)
  between operations  1.51 us (1%)
  other arithmetic  1.39 us (1%)
    ppermute x17, starting transfers between devices, swapped(): lax.ppermute(value, ('wide', 'narrow'), [(source, source ^ mask) for sour...  41.8 us
    ppermute x7, waiting for transfers between devices, shifted(): lax.ppermute(value, axis, [(source, source + steps) for source in range(f...  26.7 us
    ppermute x17, waiting for transfers between devices, swapped(): lax.ppermute(value, ('wide', 'narrow'), [(source, source ^ mask) for sour...  22.1 us
    ppermute x7, starting transfers between devices, shifted(): lax.ppermute(value, axis, [(source, source + steps) for source in range(f...  21.2 us
    pallas_call x1, Pallas kernels, run_slots(): pl.pallas_call(functools.partial(slots_kernel, tile_rows, tile_cols), out...  8.55 us
  transfers between devices with their start and end apart: 25, of which 11 were waited for; matrix products, arithmetic and copies ran while one was open for 3% of the time, Pallas kernels for 0%

profile of v1, /device:TPU:0, one launch (start us, length us, event | category | flops | bytes accessed | tf_op | source)
XLA Modules:
  0.0 131.3 jit_solution(12818482276736039872)
XLA Ops:
  0.7 2.0 %slice.49 = f32[2,256,256]{2,1,0:T(8,128)} slice(f32[2,512,256]{2,1,0:T(8,128)} %own.1), slice={[0:2], [0:256], [0:256]} | slice | bytes 1048576 | tf_op jit(solution)/shard_map/slice | solution.py:387
  2.7 1.3 collective-permute-start.1
  4.0 1.3 collective-permute-start
  5.3 1.9 %slice.50 = f32[2,256,256]{2,1,0:T(8,128)} slice(f32[2,512,256]{2,1,0:T(8,128)} %own.1), slice={[0:2], [256:512], [0:256]} | slice | bytes 1048576 | tf_op jit(solution)/shard_map/slice | solution.py:390
  7.1 1.3 collective-permute-start.2
  8.4 12.0 %collective-permute-done.1.right = f32[2,256,256]{2,1,0:T(8,128)S(1)} collective-permute-done((f32[2,256,256]{2,1,0:T(8,128)}, f32[2,256,256]{2,1,0:T(8,128)S(1)}, u32[]{:S(2)}, u32[]{:S(2)}) %collective-permute-start.1) | collective-permute-done | bytes 524320 | tf_op jit(solution)/shard_map/ppermute | solution.py:281
  20.5 1.3 collective-permute-start.3
  22.5 8.4 %collective-permute-done.2.right_low = f32[2,256,256]{2,1,0:T(8,128)S(1)} collective-permute-done((f32[2,256,256]{2,1,0:T(8,128)}, f32[2,256,256]{2,1,0:T(8,128)S(1)}, u32[]{:S(2)}, u32[]{:S(2)}) %collective-permute-start.2) | collective-permute-done | bytes 524320 | tf_op jit(solution)/shard_map/ppermute | solution.py:281
  30.9 8.5 %slots.1 = (f32[2,512,256]{2,1,0:T(8,128)S(1)}, f32[2,256,256]{2,1,0:T(8,128)S(1)}, f32[2,256,256]{2,1,0:T(8,128)S(1)}, f32[2,256,256]{2,1,0:T(8,128)S(1)}, f32[...) custom-call(s32[8,2]{1,0:T(8,128)S(1)} %copy.9.offsets, s32[1]{0:T(128)S(6)} %copy.11.live, ...), custom_call_target="tpu_custom_call" | custom-call | tf_op jit(solution)/shard_map/slots/pallas_call | solution.py:250
  40.1 9.6 %collective-permute-start.8 = (f32[2,256,256]{2,1,0:T(8,128)S(1)}, f32[2,256,256]{2,1,0:T(8,128)S(1)}, u32[]{:S(2)}, u32[]{:S(2)}) collective-permute-start(f32[2,256,256]{2,1,0:T(8,128)S(1)} %get-tuple-element.86), channel_id=1, source_target_pairs={{0,4},{4,8},{8,12},{12,16},{16,20},{20,24},{24,28},{1,5},{5,9},{9,... | collective-permute-start | bytes 1572872 | tf_op jit(solution)/shard_map/ppermute | solution.py:281
  49.8 1.2 collective-permute-start.5
  51.0 1.5 %collective-permute-start.6 = (f32[256,256]{1,0:T(8,128)S(1)}, f32[256,256]{1,0:T(8,128)S(1)}, u32[]{:S(2)}, u32[]{:S(2)}) collective-permute-start(f32[256,256]{1,0:T(8,128)S(1)} %get-tuple-element.84), channel_id=1, source_target_pairs={{0,8},{1,9},{2,10},{3,11},{4,12},{5,13},{6,14},{7,15},{8,0},{9,1},... | collective-permute-start | bytes 786440 | tf_op jit(solution)/shard_map/ppermute | solution.py:304
  52.5 0.9 collective-permute-start.7
  53.4 2.3 %collective-permute-start.15 = (f32[2,256,256]{2,1,0:T(8,128)S(1)}, f32[2,256,256]{2,1,0:T(8,128)S(1)}, u32[]{:S(2)}, u32[]{:S(2)}) collective-permute-start(f32[2,256,256]{2,1,0:T(8,128)S(1)} %get-tuple-element.100), channel_id=1, source_target_pairs={{0,4},{4,8},{8,12},{12,16},{16,20},{20,24},{24,28},{1,5},{5,9},{9,... | collective-permute-start | bytes 1572872 | tf_op jit(solution)/shard_map/ppermute | solution.py:281
  55.7 6.3 %collective-permute-done.8 = f32[2,256,256]{2,1,0:T(8,128)S(1)} collective-permute-done((f32[2,256,256]{2,1,0:T(8,128)S(1)}, f32[2,256,256]{2,1,0:T(8,128)S(1)}, u32[]{:S(2)}, u32[]{:S(2)}) %collective-permute-start.8) | collective-permute-done | bytes 524320 | tf_op jit(solution)/shard_map/ppermute | solution.py:281
  61.9 2.3 %collective-permute-start.16 = (f32[2,256,256]{2,1,0:T(8,128)S(1)}, f32[2,256,256]{2,1,0:T(8,128)S(1)}, u32[]{:S(2)}, u32[]{:S(2)}) collective-permute-start(f32[2,256,256]{2,1,0:T(8,128)S(1)} %get-tuple-element.101), channel_id=1, source_target_pairs={{0,5},{1,6},{2,7},{4,9},{5,10},{6,11},{8,13},{9,14},{10,15},{12,17... | collective-permute-start | bytes 1572872 | tf_op jit(solution)/shard_map/ppermute | solution.py:287
  64.7 4.3 %collective-permute-start.17 = (f32[2,256,256]{2,1,0:T(8,128)S(1)}, f32[2,256,256]{2,1,0:T(8,128)S(1)}, u32[]{:S(2)}, u32[]{:S(2)}) collective-permute-start(f32[2,256,256]{2,1,0:T(8,128)S(1)} %get-tuple-element.102), channel_id=1, source_target_pairs={{0,1},{1,2},{2,3},{4,5},{5,6},{6,7},{8,9},{9,10},{10,11},{12,13},{... | collective-permute-start | bytes 1572872 | tf_op jit(solution)/shard_map/ppermute | solution.py:281
  69.0 5.8 %collective-permute-start.9 = (f32[64,256]{1,0:T(8,128)S(1)}, f32[64,256]{1,0:T(8,128)S(1)}, u32[]{:S(2)}, u32[]{:S(2)}) collective-permute-start(f32[64,256]{1,0:T(8,128)S(1)} %get-tuple-element.97), channel_id=1, source_target_pairs={{0,4},{1,5},{2,6},{3,7},{4,0},{5,1},{6,2},{7,3},{8,12},{9,13},{10,... | collective-permute-start | bytes 196616 | tf_op jit(solution)/shard_map/ppermute | solution.py:304
  74.8 5.1 %collective-permute-start.10 = (f32[64,256]{1,0:T(8,128)S(1)}, f32[64,256]{1,0:T(8,128)S(1)}, u32[]{:S(2)}, u32[]{:S(2)}) collective-permute-start(f32[64,256]{1,0:T(8,128)S(1)} %get-tuple-element.98), channel_id=1, source_target_pairs={{0,16},{1,17},{2,18},{3,19},{4,20},{5,21},{6,22},{7,23},{8,24},{9,... | collective-permute-start | bytes 196616 | tf_op jit(solution)/shard_map/ppermute | solution.py:304
  79.9 5.0 %collective-permute-done.9.refs_1_ = f32[64,256]{1,0:T(8,128)S(1)} collective-permute-done((f32[64,256]{1,0:T(8,128)S(1)}, f32[64,256]{1,0:T(8,128)S(1)}, u32[]{:S(2)}, u32[]{:S(2)}) %collective-permute-start.9) | collective-permute-done | bytes 65568 | tf_op jit(solution)/shard_map/ppermute | solution.py:304
  84.9 6.0 %collective-permute-start.11 = (f32[64,256]{1,0:T(8,128)S(1)}, f32[64,256]{1,0:T(8,128)S(1)}, u32[]{:S(2)}, u32[]{:S(2)}) collective-permute-start(f32[64,256]{1,0:T(8,128)S(1)} %get-tuple-element.99), channel_id=1, source_target_pairs={{0,20},{1,21},{2,22},{3,23},{4,16},{5,17},{6,18},{7,19},{8,28},{9,... | collective-permute-start | bytes 196616 | tf_op jit(solution)/shard_map/ppermute | solution.py:304
  90.9 2.2 %collective-permute-done.11.refs_3_ = f32[64,256]{1,0:T(8,128)S(1)} collective-permute-done((f32[64,256]{1,0:T(8,128)S(1)}, f32[64,256]{1,0:T(8,128)S(1)}, u32[]{:S(2)}, u32[]{:S(2)}) %collective-permute-start.11) | collective-permute-done | bytes 65568 | tf_op jit(solution)/shard_map/ppermute | solution.py:304
  93.2 7.0 %collective-permute-start.14 = (f32[64,256]{1,0:T(8,128)S(1)}, f32[64,256]{1,0:T(8,128)S(1)}, u32[]{:S(2)}, u32[]{:S(2)}) collective-permute-start(f32[64,256]{1,0:T(8,128)S(1)} %add_parts.5.refs_0_), channel_id=1, source_target_pairs={{0,20},{1,21},{2,22},{3,23},{4,16},{5,17},{6,18},{7,19},{8,28},{9,... | collective-permute-start | bytes 196616 | tf_op jit(solution)/shard_map/ppermute | solution.py:304
  100.2 1.2 collective-permute-start.13
  101.4 1.1 collective-permute-done.14.refs_3_
  102.5 3.2 %collective-permute-start.12 = (f32[64,256]{1,0:T(8,128)S(1)}, f32[64,256]{1,0:T(8,128)S(1)}, u32[]{:S(2)}, u32[]{:S(2)}) collective-permute-start(f32[64,256]{1,0:T(8,128)S(1)} %add_parts.5.refs_0_), channel_id=1, source_target_pairs={{0,4},{1,5},{2,6},{3,7},{4,0},{5,1},{6,2},{7,3},{8,12},{9,13},{10,... | collective-permute-start | bytes 196616 | tf_op jit(solution)/shard_map/ppermute | solution.py:304
  105.7 2.2 %collective-permute-done.12.refs_1_ = f32[64,256]{1,0:T(8,128)S(1)} collective-permute-done((f32[64,256]{1,0:T(8,128)S(1)}, f32[64,256]{1,0:T(8,128)S(1)}, u32[]{:S(2)}, u32[]{:S(2)}) %collective-permute-start.12) | collective-permute-done | bytes 65568 | tf_op jit(solution)/shard_map/ppermute | solution.py:304
  108.8 6.7 %collective-permute-start.19 = (f32[256,256]{1,0:T(8,128)S(1)}, f32[256,256]{1,0:T(8,128)S(1)}, u32[]{:S(2)}, u32[]{:S(2)}) collective-permute-start(f32[256,256]{1,0:T(8,128)S(1)} %join_parts.2.refs_0_), channel_id=1, source_target_pairs={{0,8},{1,9},{2,10},{3,11},{4,12},{5,13},{6,14},{7,15},{8,0},{9,1},... | collective-permute-start | bytes 786440 | tf_op jit(solution)/shard_map/ppermute | solution.py:304
  115.5 1.4 %collective-permute-start.18 = (f32[256,256]{1,0:T(8,128)S(1)}, f32[256,256]{1,0:T(8,128)S(1)}, u32[]{:S(2)}, u32[]{:S(2)}) collective-permute-start(f32[256,256]{1,0:T(8,128)S(1)} %join_parts.2.refs_0_), channel_id=1, source_target_pairs={{0,2},{1,3},{2,0},{3,1},{4,6},{5,7},{6,4},{7,5},{8,10},{9,11},{10,... | collective-permute-start | bytes 786440 | tf_op jit(solution)/shard_map/ppermute | solution.py:304
  117.7 10.2 %collective-permute-done.19.refs_2_ = f32[256,256]{1,0:T(8,128)S(1)} collective-permute-done((f32[256,256]{1,0:T(8,128)S(1)}, f32[256,256]{1,0:T(8,128)S(1)}, u32[]{:S(2)}, u32[]{:S(2)}) %collective-permute-start.19) | collective-permute-done | bytes 262176 | tf_op jit(solution)/shard_map/ppermute | solution.py:304
  128.5 1.2 maximum_add_fusion
  129.9 1.5 %join_parts.3 = f32[2048,256]{1,0:T(8,128)} custom-call(f32[256,256]{1,0:T(8,128)S(1)} %join_parts.2.refs_0_, f32[256,256]{1,0:T(8,128)S(1)} %collective-permute-done.18.refs_1_, f32[256,256]{1,0:T(8,128)S(1)} %collective-permute-done.19.refs_2_, f32[256,256]{1,0:T(8,128)S(1)} %collective-permute-done.20.refs_3_, ...), custom_call_target="tpu_custom_call" | custom-call | tf_op jit(solution)/shard_map/join_parts/pallas_call | solution.py:342
  (38 shorter events, 3.8 us)
Async XLA Ops:
  0.6 30.2 %copy-start.2 = (bf16[256,256]{1,0:T(8,128)(2,1)S(1)}, bf16[256,256]{1,0:T(8,128)(2,1)}, u32[]{:S(2)}) copy-start(bf16[256,256]{1,0:T(8,128)(2,1)} %constant.71.order) | copy-start | bytes 393220
  0.6 30.2 %copy-start.1 = (bf16[2,2,256,256]{3,2,1,0:T(8,128)(2,1)S(1)}, bf16[2,2,256,256]{3,2,1,0:T(8,128)(2,1)}, u32[]{:S(2)}) copy-start(bf16[2,2,256,256]{3,2,1,0:T(8,128)(2,1)} %constant.66.clone.mats) | copy-start | bytes 1572868
  0.7 30.2 %copy-start = (f32[2,512,256]{2,1,0:T(8,128)S(1)}, f32[2,512,256]{2,1,0:T(8,128)}, u32[]{:S(2)}) copy-start(f32[2,512,256]{2,1,0:T(8,128)} %own.1) | copy-start | bytes 3145732
  0.7 21.7 %copy-start.3 = (s32[8,2]{0,1:T(2,128)S(1)}, s32[8,2]{0,1:T(2,128)}, u32[]{:S(2)}) copy-start(s32[8,2]{0,1:T(2,128)} %param.16) | copy-start | bytes 196
  2.7 17.8 %collective-permute-start.1 = (f32[2,256,256]{2,1,0:T(8,128)}, f32[2,256,256]{2,1,0:T(8,128)S(1)}, u32[]{:S(2)}, u32[]{:S(2)}) collective-permute-start(f32[2,256,256]{2,1,0:T(8,128)} %slice.49), channel_id=1, source_target_pairs={{4,0},{8,4},{12,8},{16,12},{20,16},{24,20},{28,24},{5,1},{9,5},{13... | collective-permute-start | bytes 1572872 | tf_op jit(solution)/shard_map/ppermute | solution.py:281
  4.0 26.9 %collective-permute-start = (f32[2,256,256]{2,1,0:T(8,128)}, f32[2,256,256]{2,1,0:T(8,128)S(1)}, u32[]{:S(2)}, u32[]{:S(2)}) collective-permute-start(f32[2,256,256]{2,1,0:T(8,128)} %slice.49), channel_id=1, source_target_pairs={{1,0},{2,1},{3,2},{5,4},{6,5},{7,6},{9,8},{10,9},{11,10},{13,12},{... | collective-permute-start | bytes 1572872 | tf_op jit(solution)/shard_map/ppermute | solution.py:281
  7.1 23.7 %collective-permute-start.2 = (f32[2,256,256]{2,1,0:T(8,128)}, f32[2,256,256]{2,1,0:T(8,128)S(1)}, u32[]{:S(2)}, u32[]{:S(2)}) collective-permute-start(f32[2,256,256]{2,1,0:T(8,128)} %slice.50), channel_id=1, source_target_pairs={{4,0},{8,4},{12,8},{16,12},{20,16},{24,20},{28,24},{5,1},{9,5},{13... | collective-permute-start | bytes 1572872 | tf_op jit(solution)/shard_map/ppermute | solution.py:281
  20.5 10.4 %collective-permute-start.3 = (f32[2,256,256]{2,1,0:T(8,128)S(1)}, f32[2,256,256]{2,1,0:T(8,128)}, u32[]{:S(2)}, u32[]{:S(2)}) collective-permute-start(f32[2,256,256]{2,1,0:T(8,128)S(1)} %collective-permute-done.1.right), channel_id=1, source_target_pairs={{1,0},{2,1},{3,2},{5,4},{6,5},{7,6},{9,8},{10,9},{11,10},{13,12},{... | collective-permute-start | bytes 1572872 | tf_op jit(solution)/shard_map/ppermute | solution.py:281
  39.5 10.2 %collective-permute-start.4 = (f32[1024,256]{1,0:T(8,128)S(1)}, f32[1024,256]{1,0:T(8,128)S(1)}, u32[]{:S(2)}, u32[]{:S(2)}) collective-permute-start(f32[1024,256]{1,0:T(8,128)S(1)} %get-tuple-element.75), channel_id=1, source_target_pairs={{0,1},{1,0},{2,3},{3,2},{4,5},{5,4},{6,7},{7,6},{8,9},{9,8},{10,11... | collective-permute-start | bytes 3145736 | tf_op jit(solution)/shard_map/ppermute | solution.py:304
  40.1 21.8 %collective-permute-start.8 = (f32[2,256,256]{2,1,0:T(8,128)S(1)}, f32[2,256,256]{2,1,0:T(8,128)S(1)}, u32[]{:S(2)}, u32[]{:S(2)}) collective-permute-start(f32[2,256,256]{2,1,0:T(8,128)S(1)} %get-tuple-element.86), channel_id=1, source_target_pairs={{0,4},{4,8},{8,12},{12,16},{16,20},{20,24},{24,28},{1,5},{5,9},{9,... | collective-permute-start | bytes 1572872 | tf_op jit(solution)/shard_map/ppermute | solution.py:281
  49.8 14.4 %collective-permute-start.5 = (f32[256,256]{1,0:T(8,128)S(1)}, f32[256,256]{1,0:T(8,128)S(1)}, u32[]{:S(2)}, u32[]{:S(2)}) collective-permute-start(f32[256,256]{1,0:T(8,128)S(1)} %get-tuple-element.83), channel_id=1, source_target_pairs={{0,2},{1,3},{2,0},{3,1},{4,6},{5,7},{6,4},{7,5},{8,10},{9,11},{10,... | collective-permute-start | bytes 786440 | tf_op jit(solution)/shard_map/ppermute | solution.py:304
  51.0 13.2 %collective-permute-start.6 = (f32[256,256]{1,0:T(8,128)S(1)}, f32[256,256]{1,0:T(8,128)S(1)}, u32[]{:S(2)}, u32[]{:S(2)}) collective-permute-start(f32[256,256]{1,0:T(8,128)S(1)} %get-tuple-element.84), channel_id=1, source_target_pairs={{0,8},{1,9},{2,10},{3,11},{4,12},{5,13},{6,14},{7,15},{8,0},{9,1},... | collective-permute-start | bytes 786440 | tf_op jit(solution)/shard_map/ppermute | solution.py:304
  52.5 12.2 %collective-permute-start.7 = (f32[256,256]{1,0:T(8,128)S(1)}, f32[256,256]{1,0:T(8,128)S(1)}, u32[]{:S(2)}, u32[]{:S(2)}) collective-permute-start(f32[256,256]{1,0:T(8,128)S(1)} %get-tuple-element.85), channel_id=1, source_target_pairs={{0,10},{1,11},{2,8},{3,9},{4,14},{5,15},{6,12},{7,13},{8,2},{9,3},... | collective-permute-start | bytes 786440 | tf_op jit(solution)/shard_map/ppermute | solution.py:304
  53.4 54.6 %collective-permute-start.15 = (f32[2,256,256]{2,1,0:T(8,128)S(1)}, f32[2,256,256]{2,1,0:T(8,128)S(1)}, u32[]{:S(2)}, u32[]{:S(2)}) collective-permute-start(f32[2,256,256]{2,1,0:T(8,128)S(1)} %get-tuple-element.100), channel_id=1, source_target_pairs={{0,4},{4,8},{8,12},{12,16},{16,20},{20,24},{24,28},{1,5},{5,9},{9,... | collective-permute-start | bytes 1572872 | tf_op jit(solution)/shard_map/ppermute | solution.py:281
  61.9 46.1 %collective-permute-start.16 = (f32[2,256,256]{2,1,0:T(8,128)S(1)}, f32[2,256,256]{2,1,0:T(8,128)S(1)}, u32[]{:S(2)}, u32[]{:S(2)}) collective-permute-start(f32[2,256,256]{2,1,0:T(8,128)S(1)} %get-tuple-element.101), channel_id=1, source_target_pairs={{0,5},{1,6},{2,7},{4,9},{5,10},{6,11},{8,13},{9,14},{10,15},{12,17... | collective-permute-start | bytes 1572872 | tf_op jit(solution)/shard_map/ppermute | solution.py:287
  64.7 43.3 %collective-permute-start.17 = (f32[2,256,256]{2,1,0:T(8,128)S(1)}, f32[2,256,256]{2,1,0:T(8,128)S(1)}, u32[]{:S(2)}, u32[]{:S(2)}) collective-permute-start(f32[2,256,256]{2,1,0:T(8,128)S(1)} %get-tuple-element.102), channel_id=1, source_target_pairs={{0,1},{1,2},{2,3},{4,5},{5,6},{6,7},{8,9},{9,10},{10,11},{12,13},{... | collective-permute-start | bytes 1572872 | tf_op jit(solution)/shard_map/ppermute | solution.py:281
  69.0 15.9 %collective-permute-start.9 = (f32[64,256]{1,0:T(8,128)S(1)}, f32[64,256]{1,0:T(8,128)S(1)}, u32[]{:S(2)}, u32[]{:S(2)}) collective-permute-start(f32[64,256]{1,0:T(8,128)S(1)} %get-tuple-element.97), channel_id=1, source_target_pairs={{0,4},{1,5},{2,6},{3,7},{4,0},{5,1},{6,2},{7,3},{8,12},{9,13},{10,... | collective-permute-start | bytes 196616 | tf_op jit(solution)/shard_map/ppermute | solution.py:304
  74.8 16.1 %collective-permute-start.10 = (f32[64,256]{1,0:T(8,128)S(1)}, f32[64,256]{1,0:T(8,128)S(1)}, u32[]{:S(2)}, u32[]{:S(2)}) collective-permute-start(f32[64,256]{1,0:T(8,128)S(1)} %get-tuple-element.98), channel_id=1, source_target_pairs={{0,16},{1,17},{2,18},{3,19},{4,20},{5,21},{6,22},{7,23},{8,24},{9,... | collective-permute-start | bytes 196616 | tf_op jit(solution)/shard_map/ppermute | solution.py:304
  84.9 8.3 %collective-permute-start.11 = (f32[64,256]{1,0:T(8,128)S(1)}, f32[64,256]{1,0:T(8,128)S(1)}, u32[]{:S(2)}, u32[]{:S(2)}) collective-permute-start(f32[64,256]{1,0:T(8,128)S(1)} %get-tuple-element.99), channel_id=1, source_target_pairs={{0,20},{1,21},{2,22},{3,23},{4,16},{5,17},{6,18},{7,19},{8,28},{9,... | collective-permute-start | bytes 196616 | tf_op jit(solution)/shard_map/ppermute | solution.py:304
  93.2 9.3 %collective-permute-start.14 = (f32[64,256]{1,0:T(8,128)S(1)}, f32[64,256]{1,0:T(8,128)S(1)}, u32[]{:S(2)}, u32[]{:S(2)}) collective-permute-start(f32[64,256]{1,0:T(8,128)S(1)} %add_parts.5.refs_0_), channel_id=1, source_target_pairs={{0,20},{1,21},{2,22},{3,23},{4,16},{5,17},{6,18},{7,19},{8,28},{9,... | collective-permute-start | bytes 196616 | tf_op jit(solution)/shard_map/ppermute | solution.py:304
  100.2 5.5 %collective-permute-start.13 = (f32[64,256]{1,0:T(8,128)S(1)}, f32[64,256]{1,0:T(8,128)S(1)}, u32[]{:S(2)}, u32[]{:S(2)}) collective-permute-start(f32[64,256]{1,0:T(8,128)S(1)} %add_parts.5.refs_0_), channel_id=1, source_target_pairs={{0,16},{1,17},{2,18},{3,19},{4,20},{5,21},{6,22},{7,23},{8,24},{9,... | collective-permute-start | bytes 196616 | tf_op jit(solution)/shard_map/ppermute | solution.py:304
  102.5 5.4 %collective-permute-start.12 = (f32[64,256]{1,0:T(8,128)S(1)}, f32[64,256]{1,0:T(8,128)S(1)}, u32[]{:S(2)}, u32[]{:S(2)}) collective-permute-start(f32[64,256]{1,0:T(8,128)S(1)} %add_parts.5.refs_0_), channel_id=1, source_target_pairs={{0,4},{1,5},{2,6},{3,7},{4,0},{5,1},{6,2},{7,3},{8,12},{9,13},{10,... | collective-permute-start | bytes 196616 | tf_op jit(solution)/shard_map/ppermute | solution.py:304
  108.0 21.6 %collective-permute-start.21 = (f32[256,256]{1,0:T(8,128)S(1)}, f32[256,256]{1,0:T(8,128)S(1)}, u32[]{:S(2)}, u32[]{:S(2)}) collective-permute-start(f32[256,256]{1,0:T(8,128)S(1)} %join_parts.2.refs_0_), channel_id=1, source_target_pairs={{0,1},{1,0},{2,3},{3,2},{4,5},{5,4},{6,7},{7,6},{8,9},{9,8},{10,11... | collective-permute-start | bytes 786440 | tf_op jit(solution)/shard_map/ppermute | solution.py:304
  108.1 9.6 %collective-permute-start.20 = (f32[256,256]{1,0:T(8,128)S(1)}, f32[256,256]{1,0:T(8,128)S(1)}, u32[]{:S(2)}, u32[]{:S(2)}) collective-permute-start(f32[256,256]{1,0:T(8,128)S(1)} %join_parts.2.refs_0_), channel_id=1, source_target_pairs={{0,10},{1,11},{2,8},{3,9},{4,14},{5,15},{6,12},{7,13},{8,2},{9,3},... | collective-permute-start | bytes 786440 | tf_op jit(solution)/shard_map/ppermute | solution.py:304
  108.8 19.2 %collective-permute-start.19 = (f32[256,256]{1,0:T(8,128)S(1)}, f32[256,256]{1,0:T(8,128)S(1)}, u32[]{:S(2)}, u32[]{:S(2)}) collective-permute-start(f32[256,256]{1,0:T(8,128)S(1)} %join_parts.2.refs_0_), channel_id=1, source_target_pairs={{0,8},{1,9},{2,10},{3,11},{4,12},{5,13},{6,14},{7,15},{8,0},{9,1},... | collective-permute-start | bytes 786440 | tf_op jit(solution)/shard_map/ppermute | solution.py:304
  115.5 12.5 %collective-permute-start.18 = (f32[256,256]{1,0:T(8,128)S(1)}, f32[256,256]{1,0:T(8,128)S(1)}, u32[]{:S(2)}, u32[]{:S(2)}) collective-permute-start(f32[256,256]{1,0:T(8,128)S(1)} %join_parts.2.refs_0_), channel_id=1, source_target_pairs={{0,2},{1,3},{2,0},{3,1},{4,6},{5,7},{6,4},{7,5},{8,10},{9,11},{10,... | collective-permute-start | bytes 786440 | tf_op jit(solution)/shard_map/ppermute | solution.py:304
  117.7 11.9 %collective-permute-start.24 = (f32[256,256]{1,0:T(8,128)S(1)}, f32[256,256]{1,0:T(8,128)S(1)}, u32[]{:S(2)}, u32[]{:S(2)}) collective-permute-start(f32[256,256]{1,0:T(8,128)S(1)} %collective-permute-done.20.refs_3_), channel_id=1, source_target_pairs={{0,1},{1,0},{2,3},{3,2},{4,5},{5,4},{6,7},{7,6},{8,9},{9,8},{10,11... | collective-permute-start | bytes 786440 | tf_op jit(solution)/shard_map/ppermute | solution.py:304
  127.9 1.7 %collective-permute-start.23 = (f32[256,256]{1,0:T(8,128)S(1)}, f32[256,256]{1,0:T(8,128)S(1)}, u32[]{:S(2)}, u32[]{:S(2)}) collective-permute-start(f32[256,256]{1,0:T(8,128)S(1)} %collective-permute-done.19.refs_2_), channel_id=1, source_target_pairs={{0,1},{1,0},{2,3},{3,2},{4,5},{5,4},{6,7},{7,6},{8,9},{9,8},{10,11... | collective-permute-start | bytes 786440 | tf_op jit(solution)/shard_map/ppermute | solution.py:304
  127.9 1.9 %collective-permute-start.22 = (f32[256,256]{1,0:T(8,128)S(1)}, f32[256,256]{1,0:T(8,128)S(1)}, u32[]{:S(2)}, u32[]{:S(2)}) collective-permute-start(f32[256,256]{1,0:T(8,128)S(1)} %collective-permute-done.18.refs_1_), channel_id=1, source_target_pairs={{0,1},{1,0},{2,3},{3,2},{4,5},{5,4},{6,7},{7,6},{8,9},{9,8},{10,11... | collective-permute-start | bytes 786440 | tf_op jit(solution)/shard_map/ppermute | solution.py:304
